TPU v7x, 32 devices: a whole 2x2x4 slice. The times are simulated.
32 devices in a mesh: section: 2 (over y), ctx: 4 (over x, core), tensor: 4 (over z).
Axes of the slice: x: 2, y: 2, z: 4, core: 2. Of those that a mesh axis runs over, the one named last changes fastest.
Arguments:
- arriving: bfloat16 [2, 1024, 4096], P('section', 'ctx', 'tensor')
- stored: bfloat16 [2, 1024, 4096], P('section', 'ctx', 'tensor')
- docs_forward: int32 [2, 1024], P('section', 'ctx'), may hold values from 0 to 3, never falling along the last dimension, each value on 1 to 512 neighbouring positions
- docs_backward: int32 [2, 1024], P('section', 'ctx'), may hold values from 0 to 3, never falling along the last dimension, each value on 1 to 512 neighbouring positions
- norm_gain: bfloat16 [2, 4096], P('section')
- query_weight: bfloat16 [2, 4096, 4096], P('section', 'ctx', 'tensor')
- key_weight: bfloat16 [2, 4096, 512], P('section', 'ctx', 'tensor')
- value_projection_weight: bfloat16 [2, 4096, 512], P('section', 'ctx', 'tensor'), may hold values from -0.09375 to 0.09375
- out_weight: bfloat16 [2, 4096, 4096], P('section', 'tensor', 'ctx'), may hold values from -0.375 to 0.375
Outputs:
- forward_output: bfloat16 [2, 1024, 4096], P('section', 'ctx', 'tensor')
- stashed: bfloat16 [2, 1024, 4096], P('section', 'ctx', 'tensor')
- rebuilt: bfloat16 [2, 1024, 4096], P('section', 'ctx', 'tensor')
Inputs may be any that keep to these rules, and one draw needn't show every extreme that they name: `docs_forward`: each row holds 4 packed documents: ids never fall, each document has 1 to 512 tokens, one exactly 512. `docs_backward`: each row holds 4 packed documents: ids never fall, each document has 1 to 512 tokens, one exactly 512.
All inputs are finite; a program needn't handle non-finite values.
Results may differ from a plain program's by a relative error of at most 0.0066.
Values may be sent and summed in bfloat16 or wider, within the bound.
A program may use at most 128 MiB of HBM per device.

v0:
```python
import math

import jax
import jax.numpy as jnp
from jax import lax
from jax.sharding import PartitionSpec as P

HEAD = 128
QH = 32
KVH = 4


norm_epsilon = 1e-05
rope_base = 500000.0


def from_partner(block, axis, distance):
    count = lax.axis_size(axis)
    route = []
    for low in range(count):
        high = low | 1 << distance
        if high != low and high < count:
            route += [(low, high), (high, low)]
    return lax.ppermute(block, axis, route)


def normalize(inputs, gain_row):
    values = inputs.astype(jnp.float32)
    mean_square = jnp.mean(values * values, axis=-1, keepdims=True)
    return (values * lax.rsqrt(mean_square + norm_epsilon) * gain_row.astype(jnp.float32)).astype(
        jnp.bfloat16
    )


def rotary(values, positions, head_size):
    half_size = head_size // 2
    tokens = values.shape[0]
    shaped = values.reshape(tokens, -1, head_size)
    exponent = jnp.arange(half_size).astype(jnp.float32) * (2.0 / head_size)
    inverse = jnp.exp(-exponent * math.log(rope_base))
    angles = positions.astype(jnp.float32)[:, None] * inverse[None, :]
    cosine_lookup = jnp.cos(angles)[:, None, :]
    sine_table = jnp.sin(angles)[:, None, :]
    first_half = shaped[:, :, :half_size]
    second_half = shaped[:, :, half_size:]
    turned = jnp.concatenate(
        (
            first_half * cosine_lookup - second_half * sine_table,
            second_half * cosine_lookup + first_half * sine_table,
        ),
        axis=2,
    )
    return turned.reshape(tokens, -1)


def attend(queries, key_rows, value_rows, query_positions, key_positions, query_docs, key_docs):
    query_count = queries.shape[0]
    key_count = key_rows.shape[0]
    group_count = key_rows.shape[1] // HEAD
    group_size = QH // KVH
    grouped = queries.reshape(query_count, group_count, group_size, HEAD)
    key_heads = key_rows.reshape(key_count, group_count, HEAD)
    value_heads = value_rows.reshape(key_count, group_count, HEAD)
    permitted_mask = (key_positions[None, :] <= query_positions[:, None]) & (
        key_docs[None, :] == query_docs[:, None]
    )
    scores = jnp.einsum(
        "qkgh,skh->kgqs", grouped, key_heads, preferred_element_type=jnp.float32
    ) * (1.0 / math.sqrt(HEAD))
    masked = jnp.where(permitted_mask[None, None], scores, -jnp.inf)
    row_peak = jnp.max(masked, axis=3, keepdims=True)
    weights = jnp.exp(masked - row_peak)
    totals = jnp.sum(weights, axis=3, keepdims=True)
    probabilities = weights.astype(jnp.bfloat16)
    mixed_heads = jnp.einsum(
        "kgqs,skh->qkgh", probabilities, value_heads, preferred_element_type=jnp.float32
    )
    mixed_heads = mixed_heads / jnp.transpose(totals, (2, 0, 1, 3))
    return mixed_heads.reshape(query_count, -1).astype(jnp.bfloat16)


def body(
    arriving,
    stored,
    docs_forward,
    docs_backward,
    norm_gain,
    query_weight,
    key_weight,
    value_projection_weight,
    out_weight,
):
    tok_rows = arriving.shape[1]
    top_bit = lax.axis_size("section").bit_length() - 2
    stashed, fetched = from_partner((arriving, stored), "section", top_bit)
    inputs = jnp.concatenate((arriving[0], fetched[0]), axis=0)
    full_rows = lax.all_gather(inputs, "tensor", axis=1, tiled=True)
    normed = normalize(full_rows, norm_gain[0])
    key_width = key_weight.shape[2]
    query_full, key_full, value_full, out_full = (
        lax.all_gather(query_weight[0], "ctx", axis=0, tiled=True),
        lax.all_gather(key_weight[0], "ctx", axis=0, tiled=True),
        lax.all_gather(value_projection_weight[0], "ctx", axis=0, tiled=True),
        lax.all_gather(out_weight[0], "ctx", axis=1, tiled=True),
    )
    query_raw = jnp.dot(normed, query_full, preferred_element_type=jnp.float32)
    key_raw = jnp.dot(normed, key_full, preferred_element_type=jnp.float32)
    value_raw = jnp.dot(normed, value_full, preferred_element_type=jnp.float32)
    offset = lax.axis_index("ctx") * tok_rows
    local_pos = offset + jnp.arange(tok_rows, dtype=jnp.int32)
    both_pos = jnp.concatenate((local_pos, local_pos), axis=0)
    queries = rotary(query_raw, both_pos, HEAD).astype(jnp.bfloat16)
    key_rows = rotary(key_raw, both_pos, HEAD).astype(jnp.bfloat16)
    value_rows = value_raw.astype(jnp.bfloat16)
    docs_pair = jnp.stack((docs_forward[0], docs_backward[0]), axis=0)
    all_keys, all_values, all_docs = (
        lax.all_gather(key_rows.reshape(2, tok_rows, key_width), "ctx", axis=1, tiled=True),
        lax.all_gather(value_rows.reshape(2, tok_rows, key_width), "ctx", axis=1, tiled=True),
        lax.all_gather(docs_pair, "ctx", axis=1, tiled=True),
    )
    key_pos = jnp.arange(all_keys.shape[1], dtype=jnp.int32)
    mixed_parts = []
    for batch_index in range(2):
        mixed_parts.append(
            attend(
                queries[batch_index * tok_rows : (batch_index + 1) * tok_rows],
                all_keys[batch_index],
                all_values[batch_index],
                local_pos,
                key_pos,
                docs_pair[batch_index],
                all_docs[batch_index],
            )
        )
    mixed_heads = jnp.concatenate(mixed_parts, axis=0)
    head_terms = jnp.dot(mixed_heads, out_full, preferred_element_type=jnp.float32)
    head_total = lax.psum_scatter(head_terms, "tensor", scatter_dimension=1, tiled=True)
    result = (inputs.astype(jnp.float32) + head_total).astype(jnp.bfloat16)
    return (result[:tok_rows][None], stashed, result[tok_rows:][None])


def solution(mesh):
    return jax.shard_map(
        body,
        mesh=mesh,
        in_specs=(
            P("section", "ctx", "tensor"),
            P("section", "ctx", "tensor"),
            P("section", "ctx"),
            P("section", "ctx"),
            P("section", None),
            P("section", "ctx", "tensor"),
            P("section", "ctx", "tensor"),
            P("section", "ctx", "tensor"),
            P("section", "tensor", "ctx"),
        ),
        out_specs=(
            P("section", "ctx", "tensor"),
            P("section", "ctx", "tensor"),
            P("section", "ctx", "tensor"),
        ),
        check_vma=False,
    )
```

profile of v0, /device:TPU:17, one launch (start us, length us, event | category | flops | bytes accessed | tf_op | source)
XLA Modules:
  0.0 429.0 jit_solution(16445038740933803226)
XLA Ops:
  7.2 0.0 all-gather.10.cloned.1.call-start
  7.2 1.3 collective-permute-start
  8.5 11.8 %collective-permute-done = bf16[1,256,1024]{2,1,0:T(8,128)(2,1)S(1)} collective-permute-done((bf16[1,256,1024]{2,1,0:T(8,128)(2,1)}, bf16[1,256,1024]{2,1,0:T(8,128)(2,1)S(1)}, u32[]{:S(2)}, u32[]{:S(2)}) %collective-permute-start) | collective-permute-done | bytes 524320 | tf_op jit(solution)/shard_map/ppermute | solution.py:24
  20.3 2.1 pad_maximum_fusion
  22.4 0.0 all-gather.14.cloned.1.call-start
  22.5 0.7 all-gather.14.cloned.1.call-update
  23.2 0.0 all-gather.12.cloned.1.call-start
  23.2 0.7 all-gather.12.cloned.1.call-update
  23.9 0.0 all-gather.16.cloned.1.call-start
  23.9 0.5 all-gather.16.cloned.1.call-update
  24.5 0.0 all-gather.18.cloned.1.call-start
  24.5 0.5 all-gather.18.cloned.1.call-update
  25.1 0.0 reduce-scatter.2.cloned.1.call-start
  25.1 0.7 mul.176
  25.9 0.7 pad_add_fusion
  26.6 6.5 %all_gather.27 = s32[2,1024]{1,0:T(2,128)S(1)} all-gather(s32[2,256]{1,0:T(2,128)S(1)} %pad_add_fusion), channel_id=1, replica_groups=mesh['section'=2,'ctx'=4,'tensor'=4] {'ctx'}, dimensions={1}, use_global_device_ids=true | all-gather | bytes 10240 | tf_op jit(solution)/shard_map/all_gather | solution.py:119
  33.1 1.0 multiply_cosine_fusion
  34.1 0.7 fusion.36
  34.8 69.0 %all-gather.10.cloned.1.call-done = bf16[512,4096]{1,0:T(8,128)(2,1)} async-done(((bf16[512,1024]{1,0:T(8,128)(2,1)}), bf16[512,4096]{1,0:T(8,128)(2,1)}) %all-gather.10.cloned.1.call-update) | async-done | bytes 4194320 | tf_op jit(solution)/shard_map/all_gather | solution.py:97
  103.8 3.1 fusion
  106.9 15.6 %all-gather.14.cloned.1.call-done = bf16[1,4096,128]{2,1,0:T(8,128)(2,1)} async-done(((bf16[1,1024,128]{2,1,0:T(8,128)(2,1)}), bf16[1,4096,128]{2,1,0:T(8,128)(2,1)}) %all-gather.14.cloned.1.call-update) | async-done | bytes 1048592 | tf_op jit(solution)/shard_map/all_gather | solution.py:102
  122.5 4.1 convolution_bitcast_fusion
  126.6 0.6 fusion.51
  127.2 0.1 copy.20
  127.3 13.5 %all-gather.12.cloned.1.call-done = bf16[1,4096,128]{2,1,0:T(8,128)(2,1)} async-done(((bf16[1,1024,128]{2,1,0:T(8,128)(2,1)}), bf16[1,4096,128]{2,1,0:T(8,128)(2,1)}) %all-gather.12.cloned.1.call-update) | async-done | bytes 1048592 | tf_op jit(solution)/shard_map/all_gather | solution.py:103
  140.8 3.8 convolution_convert_fusion
  144.6 0.1 copy.12
  144.7 7.3 %all_gather.29 = bf16[2,1024,128]{2,1,0:T(8,128)(2,1)S(1)} all-gather(bf16[2,256,128]{2,1,0:T(8,128)(2,1)S(1)} %bitcast.131), channel_id=1, replica_groups=mesh['section'=2,'ctx'=4,'tensor'=4] {'ctx'}, dimensions={1}, use_global_device_ids=true | all-gather | bytes 655360 | tf_op jit(solution)/shard_map/all_gather | solution.py:117
  152.0 10.6 %all_gather.26 = bf16[2,1024,128]{1,2,0:T(8,128)(2,1)S(1)} all-gather(bf16[2,256,128]{1,2,0:T(8,128)(2,1)S(1)} %copy.12), channel_id=1, replica_groups=mesh['section'=2,'ctx'=4,'tensor'=4] {'ctx'}, dimensions={1}, use_global_device_ids=true | all-gather | bytes 655360 | tf_op jit(solution)/shard_map/all_gather | solution.py:118
  162.7 40.7 %all-gather.16.cloned.1.call-done = bf16[1,4096,1024]{2,1,0:T(8,128)(2,1)} async-done(((bf16[1,1024,1024]{2,1,0:T(8,128)(2,1)}), bf16[1,4096,1024]{2,1,0:T(8,128)(2,1)}) %all-gather.16.cloned.1.call-update) | async-done | bytes 8388624 | tf_op jit(solution)/shard_map/all_gather | solution.py:101
  203.4 8.2 %fusion.21 = f32[64,8,8,128]{3,1,2,0:T(8,128)S(1)} fusion(bf16[1,4096,1024]{2,1,0:T(8,128)(2,1)} %all-gather.16.cloned.1.call-done, bf16[512,4096]{1,0:T(8,128)(2,1)} %all-gather.10.cloned.1.call-done, f32[4096]{0:T(1024)S(1)} %bitcast.137, f32[512]{0:T(512)S(1)} %add_rsqrt_fusion), kind=kOutput, calls=%fused_computation.28 | convolution fusion | flops 4303355904 | bytes 14698496 | tf_op jit(solution)/shard_map/dot_general | solution.py:106
  211.7 0.5 copy.23
  212.1 0.7 fusion.64
  212.8 0.8 subtract_convert_fusion
  213.6 1.6 fusion.11
  215.3 1.6 fusion.12
  216.9 3.7 fusion.7
  220.6 2.3 divide_convert_fusion.1
  222.9 2.2 divide_convert_fusion
  225.1 38.0 %all-gather.18.cloned.1.call-done = bf16[1,1024,4096]{2,1,0:T(8,128)(2,1)} async-done(((bf16[1,1024,1024]{2,1,0:T(8,128)(2,1)}), bf16[1,1024,4096]{2,1,0:T(8,128)(2,1)}) %all-gather.18.cloned.1.call-update) | async-done | bytes 8388624 | tf_op jit(solution)/shard_map/all_gather | solution.py:104
  263.1 10.2 %fusion.3 = f32[512,4096]{1,0:T(8,128)} fusion(bf16[1,1024,4096]{2,1,0:T(8,128)(2,1)} %all-gather.18.cloned.1.call-done, bf16[256,1024]{0,1:T(8,128)(2,1)S(1)} %bitcast.130, bf16[256,1024]{0,1:T(8,128)(2,1)S(1)} %bitcast.129), kind=kOutput, calls=%fused_computation.7 | convolution fusion | flops 4297064448 | bytes 17825792 | tf_op jit(solution)/shard_map/dot_general | solution.py:136
  273.4 1.0 copy-done
  274.4 1.2 collective-permute-start.1
  275.6 12.2 %collective-permute-done.1 = bf16[1,256,1024]{2,1,0:T(8,128)(2,1)S(1)} collective-permute-done((bf16[1,256,1024]{2,1,0:T(8,128)(2,1)S(1)}, bf16[1,256,1024]{2,1,0:T(8,128)(2,1)S(1)}, u32[]{:S(2)}, u32[]{:S(2)}) %collective-permute-start.1) | collective-permute-done | bytes 524320 | tf_op jit(solution)/shard_map/ppermute | solution.py:24
  287.8 130.6 %reduce-scatter.2.cloned.1.call-done = f32[512,1024]{1,0:T(8,128)} async-done(((f32[512,4096]{1,0:T(8,128)}), f32[512,1024]{1,0:T(8,128)}) %reduce-scatter.2.cloned.1.call-update) | async-done | bytes 2097168 | tf_op jit(solution)/shard_map/reduce_scatter | solution.py:137
  418.4 1.9 add_convert_fusion
  420.3 1.0 slice_bitcast_fusion
  421.4 0.8 copy.29
  (13 shorter events, 0.1 us)
Async XLA Ops:
  7.2 26.9 %copy-start.1 = (s32[1,256]{1,0:T(1,128)S(1)}, s32[1,256]{1,0:T(1,128)}, u32[]{:S(2)}) copy-start(s32[1,256]{1,0:T(1,128)} %param.11) | copy-start | bytes 3076
  7.2 26.9 %copy-start.2 = (s32[1,256]{1,0:T(1,128)S(1)}, s32[1,256]{1,0:T(1,128)}, u32[]{:S(2)}) copy-start(s32[1,256]{1,0:T(1,128)} %param.12) | copy-start | bytes 3076
  7.2 96.6 %all-gather.10.cloned.1.call-start = ((), (), s32[]{:S(2)}) async-start(), calls=%async_computation.1 | async-start | bytes 5242880 | tf_op jit(solution)/shard_map/all_gather | solution.py:97
  7.2 13.1 %collective-permute-start = (bf16[1,256,1024]{2,1,0:T(8,128)(2,1)}, bf16[1,256,1024]{2,1,0:T(8,128)(2,1)S(1)}, u32[]{:S(2)}, u32[]{:S(2)}) collective-permute-start(bf16[1,256,1024]{2,1,0:T(8,128)(2,1)} %param.10), channel_id=1, source_target_pairs={{0,16},{16,0},{1,17},{17,1},{2,18},{18,2},{3,19},{19,3},{4,20},{20... | collective-permute-start | bytes 1572872 | tf_op jit(solution)/shard_map/ppermute | solution.py:24
  22.4 100.1 %all-gather.14.cloned.1.call-start = ((), (), s32[]{:S(2)}) async-start(), calls=%async_computation.4 | async-start | bytes 1310720 | tf_op jit(solution)/shard_map/all_gather | solution.py:102
  23.2 117.7 %all-gather.12.cloned.1.call-start = ((), (), s32[]{:S(2)}) async-start(), calls=%async_computation.3 | async-start | bytes 1310720 | tf_op jit(solution)/shard_map/all_gather | solution.py:103
  23.9 179.5 %all-gather.16.cloned.1.call-start = ((), (), s32[]{:S(2)}) async-start(), calls=%async_computation.5 | async-start | bytes 10485760 | tf_op jit(solution)/shard_map/all_gather | solution.py:101
  24.5 238.7 %all-gather.18.cloned.1.call-start = ((), (), s32[]{:S(2)}) async-start(), calls=%async_computation.6 | async-start | bytes 10485760 | tf_op jit(solution)/shard_map/all_gather | solution.py:104
  25.1 393.3 %reduce-scatter.2.cloned.1.call-start = ((), (), s32[]{:S(2)}) async-start(), calls=%async_computation.2 | async-start | bytes 10485760 | tf_op jit(solution)/shard_map/reduce_scatter | solution.py:137
  273.4 1.0 copy-start
  274.4 13.4 %collective-permute-start.1 = (bf16[1,256,1024]{2,1,0:T(8,128)(2,1)S(1)}, bf16[1,256,1024]{2,1,0:T(8,128)(2,1)S(1)}, u32[]{:S(2)}, u32[]{:S(2)}) collective-permute-start(bf16[1,256,1024]{2,1,0:T(8,128)(2,1)S(1)} %copy-done), channel_id=1, source_target_pairs={{0,16},{16,0},{1,17},{17,1},{2,18},{18,2},{3,19},{19,3},{4,20},{20... | collective-permute-start | bytes 1572872 | tf_op jit(solution)/shard_map/ppermute | solution.py:24
Sparse Core Ops, SparseCore 0:
  22.5 81.1 all-gather.9
  105.3 17.1 all-gather.13
  124.1 16.7 all-gather.11
  142.2 61.1 all-gather.15
  204.8 58.2 all-gather.17
  273.5 144.8 reduce-scatter.1
where the time goes:
time: 430 us; the launch traced here: 429 us
  waiting for transfers between devices  334 us (78%)
  matrix products  34.1 us (8%)
  blocking collectives  24.4 us (6%)
  other arithmetic  15.3 us (4%)
  between operations  14.3 us (3%)
    reduce_scatter x1, waiting for transfers between devices, body(): lax.psum_scatter(head_terms, 'tensor', scatter_dimension=1, tiled=True)  131 us
    all_gather x1, waiting for transfers between devices, body(): full_rows = lax.all_gather(inputs, 'tensor', axis=1, tiled=True)  69 us
    all_gather x1, waiting for transfers between devices, body(): lax.all_gather(query_weight[0], 'ctx', axis=0, tiled=True)  40.7 us
    all_gather x1, waiting for transfers between devices, body(): lax.all_gather(out_weight[0], 'ctx', axis=1, tiled=True)  38 us
    ppermute x2, waiting for transfers between devices, from_partner(): return lax.ppermute(block, axis, route)  24 us
    all_gather x1, waiting for transfers between devices, body(): lax.all_gather(key_weight[0], 'ctx', axis=0, tiled=True)  15.6 us
    all_gather x1, waiting for transfers between devices, body(): lax.all_gather(value_projection_weight[0], 'ctx', axis=0, tiled=True)  13.5 us
    all_gather x1, blocking collectives, body(): lax.all_gather(value_rows.reshape(2, tok_rows, key_width), 'ctx', axis=1,...  10.6 us
  transfers between devices with their start and end apart: 8, of which 8 were waited for; matrix products, arithmetic and copies ran while one was open for 9% of the time, Pallas kernels for 0%

commit v1 on v0

v1 whole, which is shorter than its diff:
```python
import math

import jax
import jax.numpy as jnp
import numpy as np
from jax import lax
from jax.experimental import pallas as pl
from jax.experimental.pallas import tpu as pltpu
from jax.sharding import PartitionSpec as P

HEAD = 128
DOC_MOST = 512
norm_epsilon = 1e-05
rope_base = 500000.0
MESH = pl.DeviceIdType.MESH
F32 = jnp.float32
BF16 = jnp.bfloat16
Q_PIECES = 4
O_PIECES = 4


def layer_kernel(
    sections,
    n_ctx,
    n,
    arr,
    sto,
    docs_rows,
    docs_cols,
    gain,
    wq,
    wk,
    wv,
    wo,
    cos_all,
    sin_all,
    out_f,
    out_s,
    out_b,
    xg,
    wq_g,
    wkv_g,
    wo_g,
    normed,
    qs,
    mixed,
    kv_g,
    docs_g,
    cos_t,
    sin_t,
    pf,
    rs_out,
    rl,
    rr,
    local_sem,
    y_s,
    y_r,
    ag_s,
    ag_r,
    x_s,
    x_r,
    c_s,
    c_r,
    f_s,
    f_r,
    rs_s,
    rs_r,
):
    s = lax.axis_index("section")
    i = lax.axis_index("ctx")
    t = lax.axis_index("tensor")
    rows = arr.shape[1]
    width = arr.shape[2]
    depth = wq.shape[1]
    heads = wq.shape[2] // HEAD
    half = sections // 2
    partner = lax.rem(s + half, sections)
    across = lax.rem(i + n_ctx // 2, n_ctx)
    sibling = i + 1 - 2 * lax.rem(i, 2)
    has_left = t > 0
    has_right = t < n - 1

    barrier = pltpu.get_barrier_semaphore()
    pl.semaphore_signal(barrier, inc=1, device_id={"section": partner}, device_id_type=MESH)
    pl.semaphore_signal(barrier, inc=1, device_id={"ctx": across}, device_id_type=MESH)
    pl.semaphore_signal(barrier, inc=1, device_id={"ctx": sibling}, device_id_type=MESH)

    @pl.when(has_left)
    def _():
        pl.semaphore_signal(barrier, inc=1, device_id={"tensor": t - 1}, device_id_type=MESH)

    @pl.when(has_right)
    def _():
        pl.semaphore_signal(barrier, inc=1, device_id={"tensor": t + 1}, device_id_type=MESH)

    q_rows = depth // Q_PIECES
    o_rows = wo.shape[1] // O_PIECES
    locals_ = [
        (arr.at[0], xg.at[0, t]),
        (wk.at[0], wkv_g.at[i, :, pl.ds(0, HEAD)]),
        (wv.at[0], wkv_g.at[i, :, pl.ds(HEAD, HEAD)]),
        (wq.at[0], wq_g.at[i]),
        (wo.at[0], wo_g.at[i]),
        (docs_rows, docs_g.at[i]),
        (cos_all.at[pl.ds(pl.multiple_of(i * rows, rows), rows)], cos_t),
        (sin_all.at[pl.ds(pl.multiple_of(i * rows, rows), rows)], sin_t),
    ]
    local_copies = [
        pltpu.make_async_copy(a, b, local_sem.at[k]) for k, (a, b) in enumerate(locals_)
    ]
    for copy in local_copies:
        copy.start()

    pl.semaphore_wait(
        barrier, 3 + has_left.astype(jnp.int32) + has_right.astype(jnp.int32)
    )

    def remote(src, dst, send, recv, where):
        return pltpu.make_async_remote_copy(
            src_ref=src,
            dst_ref=dst,
            send_sem=send,
            recv_sem=recv,
            device_id=where,
            device_id_type=MESH,
        )

    pieces = [
        (docs_rows, lambda j: docs_g.at[j]),
        (wk.at[0], lambda j: wkv_g.at[j, :, pl.ds(0, HEAD)]),
        (wv.at[0], lambda j: wkv_g.at[j, :, pl.ds(HEAD, HEAD)]),
    ]
    for k in range(Q_PIECES):
        part = pl.ds(k * q_rows, q_rows)
        pieces.append((wq.at[0, part], lambda j, part=part: wq_g.at[j, part]))
    first_o = len(pieces)
    for k in range(O_PIECES):
        part = pl.ds(k * o_rows, o_rows)
        pieces.append((wo.at[0, part], lambda j, part=part: wo_g.at[j, part]))
    kv_piece = len(pieces)
    pieces.append((kv_g.at[i], lambda j: kv_g.at[j]))

    def to_across(p):
        src, slot = pieces[p]
        return remote(src, slot(i), x_s.at[p], x_r.at[p], {"ctx": across})

    def to_sibling(p):
        src, slot = pieces[p]
        return remote(src, slot(i), c_s.at[p], c_r.at[p], {"ctx": sibling})

    def passed_on(p):
        _, slot = pieces[p]
        return remote(slot(across), slot(across), f_s.at[p], f_r.at[p], {"ctx": sibling})

    def pass_on(p):
        to_across(p).wait_recv()
        passed_on(p).start()

    def arrived(p):
        to_sibling(p).wait_recv()
        passed_on(p).wait_recv()

    def ag_right(b, r):
        j = jnp.maximum(t - r, 0)
        src = arr.at[0] if (b == 0 and r == 0) else xg.at[b, j]
        return remote(src, xg.at[b, j], ag_s.at[0, b, r], ag_r.at[0, b, r], {"tensor": t + 1})

    def ag_left(b, r):
        j = jnp.minimum(t + r, n - 1)
        src = arr.at[0] if (b == 0 and r == 0) else xg.at[b, j]
        return remote(src, xg.at[b, j], ag_s.at[1, b, r], ag_r.at[1, b, r], {"tensor": t - 1})

    def sends_right(r):
        return has_right & (t >= r)

    def sends_left(r):
        return has_left & (t + r <= n - 1)

    def ag_start(b, r):
        @pl.when(sends_right(r))
        def _():
            ag_right(b, r).start()

        @pl.when(sends_left(r))
        def _():
            ag_left(b, r).start()

    def ag_wait(b, r):
        @pl.when(t - 1 - r >= 0)
        def _():
            ag_right(b, r).wait_recv()

        @pl.when(t + 1 + r <= n - 1)
        def _():
            ag_left(b, r).wait_recv()

    fetch = remote(sto.at[0], xg.at[1, t], y_s.at[0], y_r.at[0], {"section": partner})
    stash = remote(arr.at[0], out_s.at[0], y_s.at[1], y_r.at[1], {"section": partner})

    fetch.start()
    ag_start(0, 0)
    for p in range(first_o):
        to_across(p).start()
    for p in range(first_o):
        to_sibling(p).start()
    fetch.wait_recv()
    ag_start(1, 0)
    stash.start()
    for r in range(n - 2):
        for b in range(2):
            ag_wait(b, r)
            ag_start(b, r + 1)
    pass_on(0)
    pass_on(1)
    pass_on(2)
    half_q = 3 + Q_PIECES // 2
    for p in range(3, half_q):
        pass_on(p)
    for p in range(first_o, kv_piece):
        to_across(p).start()
    for copy in local_copies:
        copy.wait()

    def normalize(b):
        def step(k, carry):
            part = pl.ds(pl.multiple_of(k * 16, 16), 16)
            square = jnp.zeros((16, 1), F32)
            for j in range(n):
                v = xg[b, j, part, :].astype(F32)
                square = square + jnp.sum(v * v, axis=1, keepdims=True)
            factor = lax.rsqrt(square * (1.0 / (n * width)) + norm_epsilon)
            place = pl.ds(pl.multiple_of(b * rows + k * 16, 16), 16)
            for j in range(n):
                v = xg[b, j, part, :].astype(F32)
                g = gain[:, j * width : (j + 1) * width].astype(F32)
                normed[place, j * width : (j + 1) * width] = (v * factor * g).astype(BF16)
            return carry

        lax.fori_loop(0, rows // 16, step, 0)

    ag_wait(0, n - 2)
    normalize(0)
    for p in range(half_q, first_o):
        pass_on(p)
    for p in range(first_o, kv_piece):
        to_sibling(p).start()
    ag_wait(1, n - 2)
    normalize(1)
    for p in range(first_o):
        arrived(p)

    def rotated(u):
        both = []
        for b in range(2):
            v = u[b * rows : (b + 1) * rows]
            both.append(v * cos_t[...] + pltpu.roll(v, HEAD // 2, 1) * sin_t[...])
        return both

    k_and_v = jnp.zeros((2 * rows, 2 * HEAD), F32)
    for j in range(n_ctx):
        k_and_v = k_and_v + jnp.dot(
            normed[:, j * depth : (j + 1) * depth], wkv_g[j], preferred_element_type=F32
        )
    for b, v in enumerate(rotated(k_and_v[:, :HEAD])):
        kv_g[i, b, :, :HEAD] = v.astype(BF16)
        kv_g[i, b, :, HEAD:] = k_and_v[b * rows : (b + 1) * rows, HEAD:].astype(BF16)
    to_across(kv_piece).start()
    to_sibling(kv_piece).start()

    def q_step(c, carry):
        cols = pl.ds(pl.multiple_of(c * 2 * HEAD, 2 * HEAD), 2 * HEAD)
        acc = jnp.zeros((2 * rows, 2 * HEAD), F32)
        for j in range(n_ctx):
            acc = acc + jnp.dot(
                normed[:, j * depth : (j + 1) * depth],
                wq_g[j, :, cols],
                preferred_element_type=F32,
            )
        for h in range(2):
            place = pl.ds(pl.multiple_of((c * 2 + h) * HEAD, HEAD), HEAD)
            for b, v in enumerate(rotated(acc[:, h * HEAD : (h + 1) * HEAD])):
                qs[b * rows : (b + 1) * rows, place] = v.astype(BF16)
        return carry

    lax.fori_loop(0, heads // 2, q_step, 0)
    pass_on(kv_piece)
    for p in range(first_o, first_o + O_PIECES // 2):
        pass_on(p)
    arrived(kv_piece)

    blocks = min(n_ctx, -(-(DOC_MOST - 1) // rows) + 1)
    start = jnp.maximum(i - (blocks - 1), 0)
    keys = blocks * rows
    q_pos = i * rows + lax.broadcasted_iota(jnp.int32, (rows, keys), 0)
    k_pos = start * rows + lax.broadcasted_iota(jnp.int32, (rows, keys), 1)
    causal = k_pos <= q_pos
    for b in range(2):
        key_docs = jnp.concatenate([docs_g[start + j, b] for j in range(blocks)], axis=1)
        allowed = causal & (docs_cols[b] == key_docs[:1])
        k_b = jnp.concatenate([kv_g[start + j, b, :, :HEAD] for j in range(blocks)], axis=0)
        v_b = jnp.concatenate([kv_g[start + j, b, :, HEAD:] for j in range(blocks)], axis=0)

        def head_step(h, carry):
            place = pl.ds(pl.multiple_of(h * HEAD, HEAD), HEAD)
            q_h = qs[b * rows : (b + 1) * rows, place]
            scores = lax.dot_general(
                q_h, k_b, (((1,), (1,)), ((), ())), preferred_element_type=F32
            ) * (1.0 / math.sqrt(HEAD))
            masked = jnp.where(allowed, scores, -jnp.inf)
            peak = jnp.max(masked, axis=1, keepdims=True)
            weights = jnp.exp(masked - peak)
            total = jnp.sum(weights, axis=1, keepdims=True)
            mix = jnp.dot(weights.astype(BF16), v_b, preferred_element_type=F32)
            mixed[b * rows : (b + 1) * rows, place] = (mix / total).astype(BF16)
            return carry

        lax.fori_loop(0, heads, head_step, 0)
        if b == 0:
            pass_on(first_o + O_PIECES // 2)
    for p in range(first_o + O_PIECES // 2 + 1, kv_piece):
        pass_on(p)
    for p in range(first_o, kv_piece):
        arrived(p)

    def project(k):
        d = jnp.where(t < n // 2, n - 1 - k, k)

        def step(c, carry):
            cols = pl.ds(pl.multiple_of(c * 256, 256), 256)
            pf[d, :, cols] = jnp.dot(mixed[...], wo_g[d, :, cols], preferred_element_type=F32)
            return carry

        lax.fori_loop(0, width // 256, step, 0)

    def rs_right(r, b, d):
        return remote(
            rs_out.at[d, b], rl.at[d, b], rs_s.at[0, r, b], rs_r.at[0, r, b], {"tensor": t + 1}
        )

    def rs_left(r, b, d):
        return remote(
            rs_out.at[d, b], rr.at[d, b], rs_s.at[1, r, b], rs_r.at[1, r, b], {"tensor": t - 1}
        )

    def dest_right(r):
        return jnp.minimum(n - 1 + t - r, n - 1)

    def dest_left(r):
        return jnp.maximum(r - (n - 1 - t), 0)

    def rs_round(r):
        for b in range(2):
            part = pl.ds(b * rows, rows)

            @pl.when(has_right & (r >= t))
            def _():
                d = dest_right(r)

                @pl.when(has_left)
                def _():
                    if r > 0:
                        rs_right(r - 1, b, d).wait_recv()
                        rs_out[d, b] = (pf[d, part, :] + rl[d, b].astype(F32)).astype(BF16)

                @pl.when(jnp.logical_not(has_left))
                def _():
                    rs_out[d, b] = pf[d, part, :].astype(BF16)

                rs_right(r, b, d).start()

            @pl.when(has_left & (r >= n - 1 - t))
            def _():
                d = dest_left(r)

                @pl.when(has_right)
                def _():
                    if r > 0:
                        rs_left(r - 1, b, d).wait_recv()
                        rs_out[d, b] = (pf[d, part, :] + rr[d, b].astype(F32)).astype(BF16)

                @pl.when(jnp.logical_not(has_right))
                def _():
                    rs_out[d, b] = pf[d, part, :].astype(BF16)

                rs_left(r, b, d).start()

    for r in range(n - 1):
        project(r)
        if r == n - 2:
            project(n - 1)
        rs_round(r)

    for b, out in enumerate((out_f, out_b)):
        part = pl.ds(b * rows, rows)

        @pl.when(has_left)
        def _():
            rs_right(n - 2, b, t).wait_recv()
            pf[t, part, :] = pf[t, part, :] + rl[t, b].astype(F32)

        @pl.when(has_right)
        def _():
            rs_left(n - 2, b, t).wait_recv()
            pf[t, part, :] = pf[t, part, :] + rr[t, b].astype(F32)

        out[0] = (xg[b, t].astype(F32) + pf[t, part, :]).astype(BF16)

    stash.wait_recv()
    fetch.wait_send()
    stash.wait_send()
    for p in range(len(pieces)):
        to_across(p).wait_send()
        to_sibling(p).wait_send()
        passed_on(p).wait_send()
    for r in range(n - 1):
        for b in range(2):

            @pl.when(sends_right(r))
            def _():
                ag_right(b, r).wait_send()

            @pl.when(sends_left(r))
            def _():
                ag_left(b, r).wait_send()

            @pl.when(has_right & (r >= t))
            def _():
                rs_right(r, b, dest_right(r)).wait_send()

            @pl.when(has_left & (r >= n - 1 - t))
            def _():
                rs_left(r, b, dest_left(r)).wait_send()


def rope_tables(tokens):
    exponent = np.arange(HEAD // 2, dtype=np.float64) * (2.0 / HEAD)
    angles = np.arange(tokens, dtype=np.float64)[:, None] * rope_base ** -exponent[None, :]
    cosine, sine = np.cos(angles), np.sin(angles)
    return (
        np.concatenate((cosine, cosine), axis=1).astype(np.float32),
        np.concatenate((-sine, sine), axis=1).astype(np.float32),
    )


def solution(mesh):
    sections, n_ctx, n = (mesh.shape[a] for a in ("section", "ctx", "tensor"))

    def body(arr, sto, docs_f, docs_b, gain, wq, wk, wv, wo):
        rows, width = arr.shape[1:]
        depth, qw = wq.shape[1:]
        odepth, ow = wo.shape[1:]
        pair = jnp.stack((docs_f[0], docs_b[0]), axis=0)
        docs_rows = jnp.broadcast_to(pair[:, None, :], (2, 8, rows))
        docs_cols = pair[:, :, None]
        cosine, sine = rope_tables(rows * n_ctx)
        n_pieces = 3 + Q_PIECES + O_PIECES + 1
        hbm = pl.BlockSpec(memory_space=pl.ANY)
        vmem = pl.BlockSpec(memory_space=pltpu.VMEM)
        dma = pltpu.SemaphoreType.DMA
        block = jax.ShapeDtypeStruct((1, rows, width), BF16)

        def kernel(*refs):
            layer_kernel(sections, n_ctx, n, *refs)

        return pl.pallas_call(
            kernel,
            out_shape=(block, block, block),
            in_specs=[hbm, hbm, hbm, vmem, vmem] + [hbm] * 6,
            out_specs=(vmem, hbm, vmem),
            scratch_shapes=[
                pltpu.VMEM((2, n, rows, width), BF16),
                pltpu.VMEM((n_ctx, depth, qw), BF16),
                pltpu.VMEM((n_ctx, depth, 2 * HEAD), BF16),
                pltpu.VMEM((n_ctx, odepth, ow), BF16),
                pltpu.VMEM((2 * rows, n * width), BF16),
                pltpu.VMEM((2 * rows, qw), BF16),
                pltpu.VMEM((2 * rows, qw), BF16),
                pltpu.VMEM((n_ctx, 2, rows, 2 * HEAD), BF16),
                pltpu.VMEM((n_ctx, 2, 8, rows), jnp.int32),
                pltpu.VMEM((rows, HEAD), F32),
                pltpu.VMEM((rows, HEAD), F32),
                pltpu.VMEM((n, 2 * rows, width), F32),
                pltpu.VMEM((n, 2, rows, width), BF16),
                pltpu.VMEM((n, 2, rows, width), BF16),
                pltpu.VMEM((n, 2, rows, width), BF16),
                dma((8,)),
                dma((2,)),
                dma((2,)),
                dma((2, 2, n - 1)),
                dma((2, 2, n - 1)),
                dma((n_pieces,)),
                dma((n_pieces,)),
                dma((n_pieces,)),
                dma((n_pieces,)),
                dma((n_pieces,)),
                dma((n_pieces,)),
                dma((2, n - 1, 2)),
                dma((2, n - 1, 2)),
            ],
            compiler_params=pltpu.CompilerParams(
                collective_id=0, has_side_effects=True, vmem_limit_bytes=62 * 1024 * 1024
            ),
            cost_estimate=pl.CostEstimate(
                flops=2 * 2 * rows * n * width * (2 * qw + 2 * HEAD),
                bytes_accessed=16 * 1024 * 1024,
                transcendentals=8 * 2 * rows * 768,
            ),
            name="relay_layer",
        )(arr, sto, docs_rows, docs_cols, gain, wq, wk, wv, wo, cosine, sine)

    return jax.shard_map(
        body,
        mesh=mesh,
        in_specs=(
            P("section", "ctx", "tensor"),
            P("section", "ctx", "tensor"),
            P("section", "ctx"),
            P("section", "ctx"),
            P("section", None),
            P("section", "ctx", "tensor"),
            P("section", "ctx", "tensor"),
            P("section", "ctx", "tensor"),
            P("section", "tensor", "ctx"),
        ),
        out_specs=(
            P("section", "ctx", "tensor"),
            P("section", "ctx", "tensor"),
            P("section", "ctx", "tensor"),
        ),
        check_vma=False,
    )
```

time: 430 us -> 206 us (0.48)
  waiting for transfers between devices: 334 us -> 0 us
  Pallas kernels: 0 us -> 197 us
  matrix products: 34.1 us -> 0 us
  blocking collectives: 24.4 us -> 0 us
  other arithmetic: 15.3 us -> 0.7 us
  between operations: 14.3 us -> 0.65 us
    pallas_call x0 -> x1, Pallas kernels: none -> 197 us  [body(): pl.pallas_call(kernel, out_shape=(block, block, block), in_specs=[hbm, hb...]
    all_gather x5 -> x0, waiting for transfers between devices: 177 us -> none  [the longest x1 69 us: body(): full_rows = lax.all_gather(inputs, 'tensor', axis=1, tiled=True)]
    reduce_scatter x1 -> x0, waiting for transfers between devices: 131 us -> none  [body(): lax.psum_scatter(head_terms, 'tensor', scatter_dimension=1, tiled=True)]
    dot_general x8 -> x0, matrix products: 34.1 us -> none  [the longest x1 10.2 us: body(): jnp.dot(mixed_heads, out_full, preferred_element_type=jnp.float32)]
    all_gather x3 -> x0, blocking collectives: 24.4 us -> none  [the longest x1 10.6 us: body(): lax.all_gather(value_rows.reshape(2, tok_rows, key_width), 'ctx', axis=1,...]
    ppermute x2 -> x0, waiting for transfers between devices: 24 us -> none  [from_partner(): return lax.ppermute(block, axis, route)]
    reduce_sum x2 -> x0, other arithmetic: 6.78 us -> none  [the longest x1 3.7 us: attend(): totals = jnp.sum(weights, axis=3, keepdims=True)]
  transfers between devices with their start and end apart: 8 -> 0, of which waited for: 8 -> 0; matrix products, arithmetic and copies ran while one was open for 9% -> 0% of each run, Pallas kernels for 0% -> 0%
where the time goes in v1:
time: 206 us; the launch traced here: 205 us
  Pallas kernels  197 us (96%)
  local copies, waits for them, and re-layouts  6.06 us (3%)
    pallas_call x1, Pallas kernels, body(): pl.pallas_call(kernel, out_shape=(block, block, block), in_specs=[hbm, hb...  197 us
    unnamed x5, local copies, waits for them, and re-layouts  4.59 us

profile of v1, /device:TPU:17, one launch (start us, length us, event | category | flops | bytes accessed | tf_op | source)
XLA Modules:
  0.0 204.6 jit_solution(3370321314829597608)
XLA Ops:
  0.6 0.7 fusion
  1.3 0.6 broadcast_in_dim.4.refs_2_
  1.9 0.9 copy.14.refs_3_
  2.8 197.2 %relay_layer.1 = (bf16[1,256,1024]{2,1,0:T(8,128)(2,1)}, bf16[1,256,1024]{2,1,0:T(8,128)(2,1)}, bf16[1,256,1024]{2,1,0:T(8,128)(2,1)}) custom-call(bf16[1,256,1024]{2,1,0:T(8,128)(2,1)} %refs_0_.1, bf16[1,256,1024]{2,1,0:T(8,128)(2,1)} %refs_1_.1, s32[2,8,256]{2,1,0:T(8,128)} %broadcast_in_dim.4.refs_2_, s32[2,256,1]{2,1,0:T(8,128)} %copy.14.refs_3_, ...), custom_call_target="tpu_custom_call" | custom-call | flops 9663676416 | bytes 16777216 | tf_op jit(solution)/shard_map/relay_layer/pallas_call | solution.py:465
  200.0 0.0 copy-start
  200.0 1.9 copy.18
  202.0 1.9 copy.19
  203.8 0.0 copy-done
  203.8 0.8 copy.20
Async XLA Ops:
  200.0 3.8 %copy-start = (bf16[1,256,1024]{2,1,0:T(8,128)(2,1)S(1)}, bf16[1,256,1024]{2,1,0:T(8,128)(2,1)}, u32[]{:S(2)}) copy-start(bf16[1,256,1024]{2,1,0:T(8,128)(2,1)} %get-tuple-element.10) | copy-start | bytes 1572868

commit v2 on v1

--- a/solution.py
+++ b/solution.py
@@ -17,6 +17,7 @@
 BF16 = jnp.bfloat16
 Q_PIECES = 4
 O_PIECES = 4
+SUM_PARTS = 2
 
 
 def layer_kernel(
@@ -52,6 +53,7 @@
     rs_out,
     rl,
     rr,
+    res,
     local_sem,
     y_s,
     y_r,
@@ -74,6 +76,8 @@
     depth = wq.shape[1]
     heads = wq.shape[2] // HEAD
     half = sections // 2
+    parts_each = SUM_PARTS
+    sum_rows = rows // SUM_PARTS
     partner = lax.rem(s + half, sections)
     across = lax.rem(i + n_ctx // 2, n_ctx)
     sibling = i + 1 - 2 * lax.rem(i, 2)
@@ -138,7 +142,8 @@
         part = pl.ds(k * o_rows, o_rows)
         pieces.append((wo.at[0, part], lambda j, part=part: wo_g.at[j, part]))
     kv_piece = len(pieces)
-    pieces.append((kv_g.at[i], lambda j: kv_g.at[j]))
+    for b in range(2):
+        pieces.append((kv_g.at[i, b], lambda j, b=b: kv_g.at[j, b]))
 
     def to_across(p):
         src, slot = pieces[p]
@@ -201,7 +206,7 @@
     ag_start(0, 0)
     for p in range(first_o):
         to_across(p).start()
-    for p in range(first_o):
+    for p in range(kv_piece):
         to_sibling(p).start()
     fetch.wait_recv()
     ag_start(1, 0)
@@ -210,17 +215,6 @@
         for b in range(2):
             ag_wait(b, r)
             ag_start(b, r + 1)
-    pass_on(0)
-    pass_on(1)
-    pass_on(2)
-    half_q = 3 + Q_PIECES // 2
-    for p in range(3, half_q):
-        pass_on(p)
-    for p in range(first_o, kv_piece):
-        to_across(p).start()
-    for copy in local_copies:
-        copy.wait()
-
     def normalize(b):
         def step(k, carry):
             part = pl.ds(pl.multiple_of(k * 16, 16), 16)
@@ -238,65 +232,49 @@
 
         lax.fori_loop(0, rows // 16, step, 0)
 
-    ag_wait(0, n - 2)
-    normalize(0)
-    for p in range(half_q, first_o):
-        pass_on(p)
-    for p in range(first_o, kv_piece):
-        to_sibling(p).start()
-    ag_wait(1, n - 2)
-    normalize(1)
-    for p in range(first_o):
-        arrived(p)
-
-    def rotated(u):
-        both = []
-        for b in range(2):
-            v = u[b * rows : (b + 1) * rows]
-            both.append(v * cos_t[...] + pltpu.roll(v, HEAD // 2, 1) * sin_t[...])
-        return both
-
-    k_and_v = jnp.zeros((2 * rows, 2 * HEAD), F32)
-    for j in range(n_ctx):
-        k_and_v = k_and_v + jnp.dot(
-            normed[:, j * depth : (j + 1) * depth], wkv_g[j], preferred_element_type=F32
-        )
-    for b, v in enumerate(rotated(k_and_v[:, :HEAD])):
-        kv_g[i, b, :, :HEAD] = v.astype(BF16)
-        kv_g[i, b, :, HEAD:] = k_and_v[b * rows : (b + 1) * rows, HEAD:].astype(BF16)
-    to_across(kv_piece).start()
-    to_sibling(kv_piece).start()
-
-    def q_step(c, carry):
-        cols = pl.ds(pl.multiple_of(c * 2 * HEAD, 2 * HEAD), 2 * HEAD)
-        acc = jnp.zeros((2 * rows, 2 * HEAD), F32)
+    def rotated(v):
+        return v * cos_t[...] + pltpu.roll(v, HEAD // 2, 1) * sin_t[...]
+
+    def project_keys(b):
+        own = slice(b * rows, (b + 1) * rows)
+        k_and_v = jnp.zeros((rows, 2 * HEAD), F32)
         for j in range(n_ctx):
-            acc = acc + jnp.dot(
-                normed[:, j * depth : (j + 1) * depth],
-                wq_g[j, :, cols],
-                preferred_element_type=F32,
+            k_and_v = k_and_v + jnp.dot(
+                normed[own, j * depth : (j + 1) * depth], wkv_g[j], preferred_element_type=F32
             )
-        for h in range(2):
-            place = pl.ds(pl.multiple_of((c * 2 + h) * HEAD, HEAD), HEAD)
-            for b, v in enumerate(rotated(acc[:, h * HEAD : (h + 1) * HEAD])):
-                qs[b * rows : (b + 1) * rows, place] = v.astype(BF16)
-        return carry
-
-    lax.fori_loop(0, heads // 2, q_step, 0)
-    pass_on(kv_piece)
-    for p in range(first_o, first_o + O_PIECES // 2):
-        pass_on(p)
-    arrived(kv_piece)
+        kv_g[i, b, :, :HEAD] = rotated(k_and_v[:, :HEAD]).astype(BF16)
+        kv_g[i, b, :, HEAD:] = k_and_v[:, HEAD:].astype(BF16)
+        to_across(kv_piece + b).start()
+        to_sibling(kv_piece + b).start()
+
+    def project_queries(b):
+        own = slice(b * rows, (b + 1) * rows)
+
+        def q_step(c, carry):
+            cols = pl.ds(pl.multiple_of(c * 2 * HEAD, 2 * HEAD), 2 * HEAD)
+            acc = jnp.zeros((rows, 2 * HEAD), F32)
+            for j in range(n_ctx):
+                acc = acc + jnp.dot(
+                    normed[own, j * depth : (j + 1) * depth],
+                    wq_g[j, :, cols],
+                    preferred_element_type=F32,
+                )
+            for h in range(2):
+                place = pl.ds(pl.multiple_of((c * 2 + h) * HEAD, HEAD), HEAD)
+                qs[own, place] = rotated(acc[:, h * HEAD : (h + 1) * HEAD]).astype(BF16)
+            return carry
+
+        lax.fori_loop(0, heads // 2, q_step, 0)
 
     blocks = min(n_ctx, -(-(DOC_MOST - 1) // rows) + 1)
     start = jnp.maximum(i - (blocks - 1), 0)
     keys = blocks * rows
-    q_pos = i * rows + lax.broadcasted_iota(jnp.int32, (rows, keys), 0)
-    k_pos = start * rows + lax.broadcasted_iota(jnp.int32, (rows, keys), 1)
-    causal = k_pos <= q_pos
-    for b in range(2):
+
+    def attend(b):
+        q_pos = i * rows + lax.broadcasted_iota(jnp.int32, (rows, keys), 0)
+        k_pos = start * rows + lax.broadcasted_iota(jnp.int32, (rows, keys), 1)
         key_docs = jnp.concatenate([docs_g[start + j, b] for j in range(blocks)], axis=1)
-        allowed = causal & (docs_cols[b] == key_docs[:1])
+        allowed = (k_pos <= q_pos) & (docs_cols[b] == key_docs[:1])
         k_b = jnp.concatenate([kv_g[start + j, b, :, :HEAD] for j in range(blocks)], axis=0)
         v_b = jnp.concatenate([kv_g[start + j, b, :, HEAD:] for j in range(blocks)], axis=0)
 
@@ -315,95 +293,149 @@
             return carry
 
         lax.fori_loop(0, heads, head_step, 0)
-        if b == 0:
-            pass_on(first_o + O_PIECES // 2)
-    for p in range(first_o + O_PIECES // 2 + 1, kv_piece):
+
+    n_half = n // 2
+    x_half = i // (n_ctx // 2)
+    near = x_half * n_half
+    far = (1 - x_half) * n_half
+
+    def project(b, base):
+        own = slice(b * rows, (b + 1) * rows)
+
+        def step(c, carry):
+            d = base + c // (width // 256)
+            cols = pl.ds(pl.multiple_of(lax.rem(c, width // 256) * 256, 256), 256)
+            pf[d, own, cols] = jnp.dot(mixed[own, :], wo_g[d, :, cols], preferred_element_type=F32)
+            return carry
+
+        lax.fori_loop(0, n_half * (width // 256), step, 0)
+
+    def part_of(m):
+        return pl.ds(m * sum_rows, sum_rows)
+
+    def rs_right(d, m):
+        part = part_of(m)
+        return remote(
+            rs_out.at[d, part], rl.at[d, part], rs_s.at[0, d, m], rs_r.at[0, d, m], {"tensor": t + 1}
+        )
+
+    def rs_left(d, m):
+        part = part_of(m)
+        return remote(
+            rs_out.at[d, part], rr.at[d, part], rs_s.at[1, d, m], rs_r.at[1, d, m], {"tensor": t - 1}
+        )
+
+    def pieces_of(b):
+        return range(b * parts_each, (b + 1) * parts_each)
+
+    def first_sends(b, base):
+        for q in range(n_half):
+            low, high = base + q, base + n_half - 1 - q
+
+            @pl.when((t == n - 1) & (low < t))
+            def _():
+                for m in pieces_of(b):
+                    rs_out[low, part_of(m), :] = pf[low, part_of(m), :].astype(BF16)
+                    rs_left(low, m).start()
+
+            @pl.when((t == 0) & (high > t))
+            def _():
+                for m in pieces_of(b):
+                    rs_out[high, part_of(m), :] = pf[high, part_of(m), :].astype(BF16)
+                    rs_right(high, m).start()
+
+    def middle_sends(b, base, q):
+        low, high = base + q, base + n_half - 1 - q
+
+        @pl.when((t < n - 1) & (low < t))
+        def _():
+            for m in pieces_of(b):
+                rs_left(low, m).wait_recv()
+                rs_out[low, part_of(m), :] = (
+                    pf[low, part_of(m), :] + rr[low, part_of(m), :].astype(F32)
+                ).astype(BF16)
+                rs_left(low, m).start()
+
+        @pl.when((t > 0) & (high > t))
+        def _():
+            for m in pieces_of(b):
+                rs_right(high, m).wait_recv()
+                rs_out[high, part_of(m), :] = (
+                    pf[high, part_of(m), :] + rl[high, part_of(m), :].astype(F32)
+                ).astype(BF16)
+                rs_right(high, m).start()
+
+    for copy in local_copies:
+        copy.wait()
+    ag_wait(0, n - 2)
+    normalize(0)
+    for p in range(first_o):
         pass_on(p)
+    for p in range(first_o):
+        arrived(p)
+    project_keys(0)
+    project_queries(0)
+    pass_on(kv_piece)
+    to_across(first_o).start()
+    arrived(kv_piece)
+    attend(0)
     for p in range(first_o, kv_piece):
-        arrived(p)
-
-    def project(k):
-        d = jnp.where(t < n // 2, n - 1 - k, k)
-
-        def step(c, carry):
-            cols = pl.ds(pl.multiple_of(c * 256, 256), 256)
-            pf[d, :, cols] = jnp.dot(mixed[...], wo_g[d, :, cols], preferred_element_type=F32)
-            return carry
-
-        lax.fori_loop(0, width // 256, step, 0)
-
-    def rs_right(r, b, d):
-        return remote(
-            rs_out.at[d, b], rl.at[d, b], rs_s.at[0, r, b], rs_r.at[0, r, b], {"tensor": t + 1}
+        to_sibling(p).wait_recv()
+    project(0, near)
+    first_sends(0, near)
+
+    ag_wait(1, n - 2)
+    normalize(1)
+    project_keys(1)
+    for p in range(first_o + 1, kv_piece):
+        to_across(p).start()
+    project_queries(1)
+    pass_on(kv_piece + 1)
+    arrived(kv_piece + 1)
+    attend(1)
+    project(1, near)
+    first_sends(1, near)
+
+    for q in range(n_half):
+        middle_sends(0, near, q)
+    pass_on(first_o)
+    for p in range(first_o + 1, kv_piece):
+        pass_on(p)
+        if p - first_o - 1 < n_half:
+            middle_sends(1, near, p - first_o - 1)
+    for p in range(first_o, kv_piece):
+        passed_on(p).wait_recv()
+    for b in range(2):
+        project(b, far)
+        first_sends(b, far)
+    for b in range(2):
+        for q in range(n_half):
+            middle_sends(b, far, q)
+
+    outs = []
+    for m in range(2 * parts_each):
+        b, k = m // parts_each, m % parts_each
+        part = part_of(m)
+
+        @pl.when(has_left)
+        def _():
+            rs_right(t, m).wait_recv()
+            pf[t, part, :] = pf[t, part, :] + rl[t, part, :].astype(F32)
+
+        @pl.when(has_right)
+        def _():
+            rs_left(t, m).wait_recv()
+            pf[t, part, :] = pf[t, part, :] + rr[t, part, :].astype(F32)
+
+        own = pl.ds(k * sum_rows, sum_rows)
+        res[part, :] = (xg[b, t, own, :].astype(F32) + pf[t, part, :]).astype(BF16)
+        out = pltpu.make_async_copy(
+            res.at[part], (out_f, out_b)[b].at[0, own], local_sem.at[len(locals_) + m]
         )
-
-    def rs_left(r, b, d):
-        return remote(
-            rs_out.at[d, b], rr.at[d, b], rs_s.at[1, r, b], rs_r.at[1, r, b], {"tensor": t - 1}
-        )
-
-    def dest_right(r):
-        return jnp.minimum(n - 1 + t - r, n - 1)
-
-    def dest_left(r):
-        return jnp.maximum(r - (n - 1 - t), 0)
-
-    def rs_round(r):
-        for b in range(2):
-            part = pl.ds(b * rows, rows)
-
-            @pl.when(has_right & (r >= t))
-            def _():
-                d = dest_right(r)
-
-                @pl.when(has_left)
-                def _():
-                    if r > 0:
-                        rs_right(r - 1, b, d).wait_recv()
-                        rs_out[d, b] = (pf[d, part, :] + rl[d, b].astype(F32)).astype(BF16)
-
-                @pl.when(jnp.logical_not(has_left))
-                def _():
-                    rs_out[d, b] = pf[d, part, :].astype(BF16)
-
-                rs_right(r, b, d).start()
-
-            @pl.when(has_left & (r >= n - 1 - t))
-            def _():
-                d = dest_left(r)
-
-                @pl.when(has_right)
-                def _():
-                    if r > 0:
-                        rs_left(r - 1, b, d).wait_recv()
-                        rs_out[d, b] = (pf[d, part, :] + rr[d, b].astype(F32)).astype(BF16)
-
-                @pl.when(jnp.logical_not(has_right))
-                def _():
-                    rs_out[d, b] = pf[d, part, :].astype(BF16)
-
-                rs_left(r, b, d).start()
-
-    for r in range(n - 1):
-        project(r)
-        if r == n - 2:
-            project(n - 1)
-        rs_round(r)
-
-    for b, out in enumerate((out_f, out_b)):
-        part = pl.ds(b * rows, rows)
-
-        @pl.when(has_left)
-        def _():
-            rs_right(n - 2, b, t).wait_recv()
-            pf[t, part, :] = pf[t, part, :] + rl[t, b].astype(F32)
-
-        @pl.when(has_right)
-        def _():
-            rs_left(n - 2, b, t).wait_recv()
-            pf[t, part, :] = pf[t, part, :] + rr[t, b].astype(F32)
-
-        out[0] = (xg[b, t].astype(F32) + pf[t, part, :]).astype(BF16)
+        out.start()
+        outs.append(out)
+    for out in outs:
+        out.wait()
 
     stash.wait_recv()
     fetch.wait_send()
@@ -423,13 +455,17 @@
             def _():
                 ag_left(b, r).wait_send()
 
-            @pl.when(has_right & (r >= t))
-            def _():
-                rs_right(r, b, dest_right(r)).wait_send()
-
-            @pl.when(has_left & (r >= n - 1 - t))
-            def _():
-                rs_left(r, b, dest_left(r)).wait_send()
+    for d in range(n):
+
+        @pl.when(d > t)
+        def _():
+            for m in range(2 * parts_each):
+                rs_right(d, m).wait_send()
+
+        @pl.when(d < t)
+        def _():
+            for m in range(2 * parts_each):
+                rs_left(d, m).wait_send()
 
 
 def rope_tables(tokens):
@@ -453,7 +489,7 @@
         docs_rows = jnp.broadcast_to(pair[:, None, :], (2, 8, rows))
         docs_cols = pair[:, :, None]
         cosine, sine = rope_tables(rows * n_ctx)
-        n_pieces = 3 + Q_PIECES + O_PIECES + 1
+        n_pieces = 3 + Q_PIECES + O_PIECES + 2
         hbm = pl.BlockSpec(memory_space=pl.ANY)
         vmem = pl.BlockSpec(memory_space=pltpu.VMEM)
         dma = pltpu.SemaphoreType.DMA
@@ -466,7 +502,7 @@
             kernel,
             out_shape=(block, block, block),
             in_specs=[hbm, hbm, hbm, vmem, vmem] + [hbm] * 6,
-            out_specs=(vmem, hbm, vmem),
+            out_specs=(hbm, hbm, hbm),
             scratch_shapes=[
                 pltpu.VMEM((2, n, rows, width), BF16),
                 pltpu.VMEM((n_ctx, depth, qw), BF16),
@@ -480,10 +516,11 @@
                 pltpu.VMEM((rows, HEAD), F32),
                 pltpu.VMEM((rows, HEAD), F32),
                 pltpu.VMEM((n, 2 * rows, width), F32),
-                pltpu.VMEM((n, 2, rows, width), BF16),
-                pltpu.VMEM((n, 2, rows, width), BF16),
-                pltpu.VMEM((n, 2, rows, width), BF16),
-                dma((8,)),
+                pltpu.VMEM((n, 2 * rows, width), BF16),
+                pltpu.VMEM((n, 2 * rows, width), BF16),
+                pltpu.VMEM((n, 2 * rows, width), BF16),
+                pltpu.VMEM((2 * rows, width), BF16),
+                dma((8 + 2 * SUM_PARTS,)),
                 dma((2,)),
                 dma((2,)),
                 dma((2, 2, n - 1)),
@@ -494,8 +531,8 @@
                 dma((n_pieces,)),
                 dma((n_pieces,)),
                 dma((n_pieces,)),
-                dma((2, n - 1, 2)),
-                dma((2, n - 1, 2)),
+                dma((2, n, 2 * SUM_PARTS)),
+                dma((2, n, 2 * SUM_PARTS)),
             ],
             compiler_params=pltpu.CompilerParams(
                 collective_id=0, has_side_effects=True, vmem_limit_bytes=62 * 1024 * 1024

time: 206 us -> 195 us (0.947)
  Pallas kernels: 197 us -> 187 us
    pallas_call x1, Pallas kernels: 197 us -> 187 us  [body(): pl.pallas_call(kernel, out_shape=(block, block, block), in_specs=[hbm, hb...]
where the time goes in v2:
time: 195 us
  Pallas kernels  187 us (96%)
  local copies, waits for them, and re-layouts  6.06 us (3%)
    pallas_call x1, Pallas kernels, body(): pl.pallas_call(kernel, out_shape=(block, block, block), in_specs=[hbm, hb...  187 us
    unnamed x5, local copies, waits for them, and re-layouts  4.59 us

profile of v2, /device:TPU:17, one launch (start us, length us, event | category | flops | bytes accessed | tf_op | source)
XLA Modules:
  0.0 194.8 jit_solution(5865712369898024328)
XLA Ops:
  0.6 0.7 fusion
  1.3 0.6 broadcast_in_dim.4.refs_2_
  1.9 0.9 copy.14.refs_3_
  2.8 187.4 %relay_layer.1 = (bf16[1,256,1024]{2,1,0:T(8,128)(2,1)}, bf16[1,256,1024]{2,1,0:T(8,128)(2,1)}, bf16[1,256,1024]{2,1,0:T(8,128)(2,1)}) custom-call(bf16[1,256,1024]{2,1,0:T(8,128)(2,1)} %refs_0_.1, bf16[1,256,1024]{2,1,0:T(8,128)(2,1)} %refs_1_.1, s32[2,8,256]{2,1,0:T(8,128)} %broadcast_in_dim.4.refs_2_, s32[2,256,1]{2,1,0:T(8,128)} %copy.14.refs_3_, ...), custom_call_target="tpu_custom_call" | custom-call | flops 9663676416 | bytes 16777216 | tf_op jit(solution)/shard_map/relay_layer/pallas_call | solution.py:501
  190.2 0.0 copy-start
  190.2 1.9 copy.18
  192.1 1.9 copy.19
  194.0 0.0 copy-done
  194.0 0.8 copy.20
Async XLA Ops:
  190.2 3.8 %copy-start = (bf16[1,256,1024]{2,1,0:T(8,128)(2,1)S(1)}, bf16[1,256,1024]{2,1,0:T(8,128)(2,1)}, u32[]{:S(2)}) copy-start(bf16[1,256,1024]{2,1,0:T(8,128)(2,1)} %get-tuple-element.10) | copy-start | bytes 1572868

commit v3 on v2

--- a/solution.py
+++ b/solution.py
@@ -145,7 +145,26 @@
     for b in range(2):
         pieces.append((kv_g.at[i, b], lambda j, b=b: kv_g.at[j, b]))
 
+    x_half = i // (n_ctx // 2)
+    first_own = jnp.where(x_half == 0, 0, n_ctx - 1)
+    first_far = jnp.where(x_half == 0, n_ctx - 1, 0)
+    second_own = jnp.where(x_half == 0, 1, n_ctx - 2)
+    second_far = jnp.where(x_half == 0, n_ctx - 2, 1)
+    per_slot = O_PIECES // 2
+
+    def out_piece(p, far):
+        k, w = (p - first_o) // per_slot, (p - first_o) % per_slot
+        place = pl.multiple_of((lax.rem(i, 2) * per_slot + w) * o_rows, o_rows)
+        slot = ((first_own, second_own), (first_far, second_far))[far][k]
+        return wo_g.at[slot, pl.ds(place, o_rows)]
+
+    def is_out(p):
+        return first_o <= p < kv_piece
+
     def to_across(p):
+        if is_out(p):
+            ref = out_piece(p, 0)
+            return remote(ref, ref, x_s.at[p], x_r.at[p], {"ctx": across})
         src, slot = pieces[p]
         return remote(src, slot(i), x_s.at[p], x_r.at[p], {"ctx": across})
 
@@ -154,6 +173,9 @@
         return remote(src, slot(i), c_s.at[p], c_r.at[p], {"ctx": sibling})
 
     def passed_on(p):
+        if is_out(p):
+            ref = out_piece(p, 1)
+            return remote(ref, ref, f_s.at[p], f_r.at[p], {"ctx": sibling})
         _, slot = pieces[p]
         return remote(slot(across), slot(across), f_s.at[p], f_r.at[p], {"ctx": sibling})
 
@@ -295,11 +317,9 @@
         lax.fori_loop(0, heads, head_step, 0)
 
     n_half = n // 2
-    x_half = i // (n_ctx // 2)
     near = x_half * n_half
-    far = (1 - x_half) * n_half
-
-    def project(b, base):
+
+    def project(b, base, count):
         own = slice(b * rows, (b + 1) * rows)
 
         def step(c, carry):
@@ -308,7 +328,7 @@
             pf[d, own, cols] = jnp.dot(mixed[own, :], wo_g[d, :, cols], preferred_element_type=F32)
             return carry
 
-        lax.fori_loop(0, n_half * (width // 256), step, 0)
+        lax.fori_loop(0, count * (width // 256), step, 0)
 
     def part_of(m):
         return pl.ds(m * sum_rows, sum_rows)
@@ -328,9 +348,9 @@
     def pieces_of(b):
         return range(b * parts_each, (b + 1) * parts_each)
 
-    def first_sends(b, base):
-        for q in range(n_half):
-            low, high = base + q, base + n_half - 1 - q
+    def first_sends(b, base, count):
+        for q in range(count):
+            low, high = base + q, base + count - 1 - q
 
             @pl.when((t == n - 1) & (low < t))
             def _():
@@ -344,8 +364,8 @@
                     rs_out[high, part_of(m), :] = pf[high, part_of(m), :].astype(BF16)
                     rs_right(high, m).start()
 
-    def middle_sends(b, base, q):
-        low, high = base + q, base + n_half - 1 - q
+    def middle_sends(b, base, count, q):
+        low, high = base + q, base + count - 1 - q
 
         @pl.when((t < n - 1) & (low < t))
         def _():
@@ -374,43 +394,51 @@
     for p in range(first_o):
         arrived(p)
     project_keys(0)
+    for p in range(first_o, kv_piece):
+        to_sibling(p).wait_recv()
+    for p in range(first_o, first_o + per_slot):
+        to_across(p).start()
     project_queries(0)
     pass_on(kv_piece)
-    to_across(first_o).start()
     arrived(kv_piece)
     attend(0)
-    for p in range(first_o, kv_piece):
-        to_sibling(p).wait_recv()
-    project(0, near)
-    first_sends(0, near)
+    project(0, near, n_half)
+    first_sends(0, near, n_half)
 
     ag_wait(1, n - 2)
     normalize(1)
     project_keys(1)
-    for p in range(first_o + 1, kv_piece):
+    for p in range(first_o + per_slot, kv_piece):
         to_across(p).start()
     project_queries(1)
     pass_on(kv_piece + 1)
     arrived(kv_piece + 1)
     attend(1)
-    project(1, near)
-    first_sends(1, near)
-
+    project(1, near, n_half)
+    first_sends(1, near, n_half)
+
+    for p in range(first_o, first_o + per_slot):
+        pass_on(p)
     for q in range(n_half):
-        middle_sends(0, near, q)
-    pass_on(first_o)
-    for p in range(first_o + 1, kv_piece):
-        pass_on(p)
-        if p - first_o - 1 < n_half:
-            middle_sends(1, near, p - first_o - 1)
-    for p in range(first_o, kv_piece):
+        middle_sends(0, near, n_half, q)
+    for p in range(first_o, first_o + per_slot):
         passed_on(p).wait_recv()
     for b in range(2):
-        project(b, far)
-        first_sends(b, far)
+        project(b, first_far, 1)
+        first_sends(b, first_far, 1)
+    middle_sends(1, near, n_half, 0)
+    for p in range(first_o + per_slot, kv_piece):
+        pass_on(p)
+    for q in range(1, n_half):
+        middle_sends(1, near, n_half, q)
+    for p in range(first_o + per_slot, kv_piece):
+        passed_on(p).wait_recv()
     for b in range(2):
-        for q in range(n_half):
-            middle_sends(b, far, q)
+        project(b, second_far, 1)
+        first_sends(b, second_far, 1)
+    for d in (first_far, second_far):
+        for b in range(2):
+            middle_sends(b, d, 1, 0)
 
     outs = []
     for m in range(2 * parts_each):

time: 195 us -> 199 us (1.021)
  Pallas kernels: 187 us -> 191 us
    pallas_call x1, Pallas kernels: 187 us -> 191 us  [body(): pl.pallas_call(kernel, out_shape=(block, block, block), in_specs=[hbm, hb...]
where the time goes in v3:
time: 199 us
  Pallas kernels  191 us (96%)
  local copies, waits for them, and re-layouts  6.06 us (3%)
    pallas_call x1, Pallas kernels, body(): pl.pallas_call(kernel, out_shape=(block, block, block), in_specs=[hbm, hb...  191 us
    unnamed x5, local copies, waits for them, and re-layouts  4.59 us

profile of v3, /device:TPU:17, one launch (start us, length us, event | category | flops | bytes accessed | tf_op | source)
XLA Modules:
  0.0 198.9 jit_solution(15105386498779871796)
XLA Ops:
  0.6 0.7 fusion
  1.3 0.6 broadcast_in_dim.4.refs_2_
  1.9 0.9 copy.14.refs_3_
  2.8 191.4 %relay_layer.1 = (bf16[1,256,1024]{2,1,0:T(8,128)(2,1)}, bf16[1,256,1024]{2,1,0:T(8,128)(2,1)}, bf16[1,256,1024]{2,1,0:T(8,128)(2,1)}) custom-call(bf16[1,256,1024]{2,1,0:T(8,128)(2,1)} %refs_0_.1, bf16[1,256,1024]{2,1,0:T(8,128)(2,1)} %refs_1_.1, s32[2,8,256]{2,1,0:T(8,128)} %broadcast_in_dim.4.refs_2_, s32[2,256,1]{2,1,0:T(8,128)} %copy.14.refs_3_, ...), custom_call_target="tpu_custom_call" | custom-call | flops 9663676416 | bytes 16777216 | tf_op jit(solution)/shard_map/relay_layer/pallas_call | solution.py:529
  194.3 0.0 copy-start
  194.3 1.9 copy.18
  196.2 1.9 copy.19
  198.1 0.0 copy-done
  198.1 0.8 copy.20
Async XLA Ops:
  194.3 3.8 %copy-start = (bf16[1,256,1024]{2,1,0:T(8,128)(2,1)S(1)}, bf16[1,256,1024]{2,1,0:T(8,128)(2,1)}, u32[]{:S(2)}) copy-start(bf16[1,256,1024]{2,1,0:T(8,128)(2,1)} %get-tuple-element.10) | copy-start | bytes 1572868

commit v4 on v2

--- a/solution.py
+++ b/solution.py
@@ -376,7 +376,8 @@
     project_keys(0)
     project_queries(0)
     pass_on(kv_piece)
-    to_across(first_o).start()
+    for p in range(first_o, first_o + O_PIECES // 2):
+        to_across(p).start()
     arrived(kv_piece)
     attend(0)
     for p in range(first_o, kv_piece):
@@ -387,7 +388,7 @@
     ag_wait(1, n - 2)
     normalize(1)
     project_keys(1)
-    for p in range(first_o + 1, kv_piece):
+    for p in range(first_o + O_PIECES // 2, kv_piece):
         to_across(p).start()
     project_queries(1)
     pass_on(kv_piece + 1)

time: 195 us -> 205 us (1.051)
  Pallas kernels: 187 us -> 197 us
    pallas_call x1, Pallas kernels: 187 us -> 197 us  [body(): pl.pallas_call(kernel, out_shape=(block, block, block), in_specs=[hbm, hb...]
where the time goes in v4:
time: 205 us
  Pallas kernels  197 us (96%)
  local copies, waits for them, and re-layouts  6.06 us (3%)
    pallas_call x1, Pallas kernels, body(): pl.pallas_call(kernel, out_shape=(block, block, block), in_specs=[hbm, hb...  197 us
    unnamed x5, local copies, waits for them, and re-layouts  4.59 us

profile of v4, /device:TPU:17, one launch (start us, length us, event | category | flops | bytes accessed | tf_op | source)
XLA Modules:
  0.0 204.8 jit_solution(4703993599536623746)
XLA Ops:
  0.6 0.7 fusion
  1.3 0.6 broadcast_in_dim.4.refs_2_
  1.9 0.9 copy.14.refs_3_
  2.8 197.3 %relay_layer.1 = (bf16[1,256,1024]{2,1,0:T(8,128)(2,1)}, bf16[1,256,1024]{2,1,0:T(8,128)(2,1)}, bf16[1,256,1024]{2,1,0:T(8,128)(2,1)}) custom-call(bf16[1,256,1024]{2,1,0:T(8,128)(2,1)} %refs_0_.1, bf16[1,256,1024]{2,1,0:T(8,128)(2,1)} %refs_1_.1, s32[2,8,256]{2,1,0:T(8,128)} %broadcast_in_dim.4.refs_2_, s32[2,256,1]{2,1,0:T(8,128)} %copy.14.refs_3_, ...), custom_call_target="tpu_custom_call" | custom-call | flops 9663676416 | bytes 16777216 | tf_op jit(solution)/shard_map/relay_layer/pallas_call | solution.py:502
  200.2 0.0 copy-start
  200.2 1.9 copy.18
  202.1 1.9 copy.19
  204.0 0.0 copy-done
  204.0 0.8 copy.20
Async XLA Ops:
  200.2 3.8 %copy-start = (bf16[1,256,1024]{2,1,0:T(8,128)(2,1)S(1)}, bf16[1,256,1024]{2,1,0:T(8,128)(2,1)}, u32[]{:S(2)}) copy-start(bf16[1,256,1024]{2,1,0:T(8,128)(2,1)} %get-tuple-element.10) | copy-start | bytes 1572868
